TPU v7x, 512 devices: a whole 4x4x16 slice. The times are simulated.
512 devices in a mesh: ctx: 32 (over z, core), exp: 16 (over y, x).
Axes of the slice: x: 4, y: 4, z: 16, core: 2. Of those that a mesh axis runs over, the one named last changes fastest.
Arguments:
- x_in: bfloat16 [4096, 4096], P('ctx', 'exp'), may hold values from -6 to 6
- z_gate: bfloat16 [4096, 4096], P('ctx', 'exp'), may hold values from -6 to 6
- b_proj: bfloat16 [4096, 128], P('ctx'), may hold values from -0.5 to 0.5
- c_proj: bfloat16 [4096, 128], P('ctx'), may hold values from -0.5 to 0.5
- dt_raw: float32 [64, 4096], P('exp', 'ctx'), may hold values from -4 to 4
- a_log: float32 [64], P('exp'), may hold values from -13 to -2.9
- d_skip: float32 [64], P('exp'), may hold values from 0.5 to 1.5
- out_proj: bfloat16 [4096, 2048], P('exp'), may hold values from -0.09375 to 0.09375
- residual: bfloat16 [4096, 2048], P('ctx'), may hold values from -80 to 80
- norm_gain: float32 [2048], replicated, may hold values from 0.5 to 1.5
- router: bfloat16 [2048, 16], replicated, may hold values from -0.125 to 0.125
- w_gate: bfloat16 [16, 2048, 7168], P(None, 'ctx', 'exp'), may hold values from -0.125 to 0.125
- w_up: bfloat16 [16, 2048, 7168], P(None, 'ctx', 'exp'), may hold values from -0.125 to 0.125
- w_down: bfloat16 [16, 2048, 7168], P(None, 'ctx', 'exp'), may hold values from -0.0625 to 0.0625
- block_experts: int32 [32, 2], replicated, may hold values from 0 to 15, all different within a row
Outputs:
- stream_out: bfloat16 [4096, 2048], P('ctx', 'exp')
- expert_out: bfloat16 [4096, 2048], P('ctx', 'exp')
All inputs are finite; a program needn't handle non-finite values.
Results may differ from a plain program's by a relative error of at most 0.03.
Values may be sent and summed in bfloat16 or wider, within the bound.
A program may use at most 64 MiB of HBM per device.

v0:
```python
import jax
import jax.numpy as jnp
from jax import lax
from jax.sharding import PartitionSpec as P

BLOCK = 128
highest = lax.Precision.HIGHEST
epsilon = 1e-05


def shifted(shard, axis, by):
    size = lax.axis_size(axis)
    pairs = [(i, i + by) for i in range(size) if 0 <= i + by < size]
    return lax.ppermute(shard, axis, pairs)


def block_terms(inputs_f, steps_f, keys_f, queries_f, head_rates):
    length = inputs_f.shape[0]
    log_decay = -head_rates[:, None] * steps_f
    running = jnp.cumsum(log_decay, axis=1)
    spread = running[:, :, None] - running[:, None, :]
    lower_part = jnp.arange(length)[:, None] >= jnp.arange(length)[None, :]
    weights = jnp.where(lower_part[None], jnp.exp(jnp.minimum(spread, 0.0)), 0.0)
    scores = jnp.dot(queries_f, keys_f.T, precision=highest)
    mixing = scores[None] * weights * steps_f[:, None, :]
    inside = jnp.einsum("hls,shp->lhp", mixing, inputs_f, precision=highest)
    carry_weight = jnp.exp(running[:, -1:] - running) * steps_f
    own_state = jnp.einsum("hs,shp,sn->hpn", carry_weight, inputs_f, keys_f, precision=highest)
    return (inside, own_state, jnp.exp(running), jnp.exp(running[:, -1]))


def per_device(
    x_in,
    z_gate,
    b_proj,
    c_proj,
    dt_raw,
    a_log,
    d_skip,
    out_proj,
    residual,
    norm_gain,
    router,
    w_gate,
    w_up,
    w_down,
    block_experts,
):
    slab_rows = x_in.shape[0]
    head_count = dt_raw.shape[0]
    head_size = x_in.shape[1] // head_count
    blocks_here = slab_rows // BLOCK
    head_rates = jnp.exp(a_log)
    steps_f = jax.nn.softplus(dt_raw).reshape(head_count, blocks_here, BLOCK).transpose(1, 0, 2)
    inputs_f = x_in.astype(jnp.float32).reshape(blocks_here, BLOCK, head_count, head_size)
    keys_f = b_proj.astype(jnp.float32).reshape(blocks_here, BLOCK, -1)
    queries_f = c_proj.astype(jnp.float32).reshape(blocks_here, BLOCK, -1)
    inside, own_state, entry_scale, block_decay = jax.vmap(block_terms, in_axes=(0, 0, 0, 0, None))(
        inputs_f, steps_f, keys_f, queries_f, head_rates
    )
    partial_states = []
    slab_keep = jnp.ones((head_count,), jnp.float32)
    slab_state = jnp.zeros(own_state.shape[1:], jnp.float32)
    kept_decay = slab_keep
    partial_states.append(slab_state)
    slab_state = block_decay[0][:, None, None] * slab_state + own_state[0]
    slab_keep = slab_keep * block_decay[0]

    def relay(turn, arriving):
        return shifted(
            (slab_keep[:, None, None] * arriving + slab_state).astype(jnp.bfloat16), "ctx", 1
        ).astype(jnp.float32)

    incoming = lax.fori_loop(0, lax.axis_size("ctx") - 1, relay, jnp.zeros_like(slab_state))
    entering = jnp.stack([kept_decay[:, None, None] * incoming])
    from_before = entry_scale.transpose(0, 2, 1)[..., None] * jnp.einsum(
        "bln,bhpn->blhp", queries_f, entering, precision=highest
    )
    outputs = inside + from_before + d_skip[None, None, :, None] * inputs_f
    gated_rows = (outputs.reshape(slab_rows, -1) * jax.nn.silu(z_gate.astype(jnp.float32))).astype(
        jnp.bfloat16
    )
    group_term = jnp.dot(gated_rows, out_proj, preferred_element_type=jnp.float32).astype(
        jnp.bfloat16
    )
    model_width = residual.shape[1]
    share_cols = model_width // lax.axis_size("exp")
    first_col = lax.axis_index("exp") * share_cols
    mixed_sum = lax.psum(group_term, "exp").astype(jnp.float32)
    stream_full = mixed_sum + residual.astype(jnp.float32)
    mean_square = jnp.mean(stream_full * stream_full, axis=1, keepdims=True)
    normed = (stream_full * lax.rsqrt(mean_square + epsilon) * norm_gain).astype(jnp.bfloat16)
    stream_share = lax.dynamic_slice_in_dim(stream_full, first_col, share_cols, 1)
    expert_count = router.shape[1]
    logits = jnp.dot(normed, router, preferred_element_type=jnp.float32).reshape(
        blocks_here, BLOCK, expert_count
    )
    named_here = lax.dynamic_slice_in_dim(
        block_experts, lax.axis_index("ctx") * blocks_here, blocks_here, 0
    )
    one_hot = (
        named_here[:, :, None] == jnp.arange(expert_count, dtype=jnp.int32)[None, None, :]
    ).astype(jnp.float32)
    chosen = jnp.einsum("bte,bse->bts", logits, one_hot, precision=highest)
    mixing_gates = jax.nn.sigmoid(chosen - chosen[:, :, ::-1])
    flat_named = block_experts.reshape(-1)
    sent_gate = jnp.take(w_gate, flat_named, axis=0)
    sent_up = jnp.take(w_up, flat_named, axis=0)
    sent_down = jnp.take(w_down, flat_named, axis=0)
    got_gate, got_up, got_down = (
        lax.all_to_all(sent_gate, "ctx", split_axis=0, concat_axis=1, tiled=True),
        lax.all_to_all(sent_up, "ctx", split_axis=0, concat_axis=1, tiled=True),
        lax.all_to_all(sent_down, "ctx", split_axis=0, concat_axis=1, tiled=True),
    )
    full_gate = got_gate.reshape(blocks_here, 2, model_width, -1)
    full_up = got_up.reshape(blocks_here, 2, model_width, -1)
    full_down = got_down.reshape(blocks_here, 2, model_width, -1)
    rows_in = normed.reshape(blocks_here, BLOCK, model_width)
    gate_part = jnp.einsum("btd,bkdf->bktf", rows_in, full_gate, preferred_element_type=jnp.float32)
    up_part = jnp.einsum("btd,bkdf->bktf", rows_in, full_up, preferred_element_type=jnp.float32)
    hidden = (jax.nn.silu(gate_part) * up_part).astype(jnp.bfloat16)
    down_part = jnp.einsum("bktf,bkdf->bktd", hidden, full_down, preferred_element_type=jnp.float32)
    weighted = jnp.sum(mixing_gates.transpose(0, 2, 1)[..., None] * down_part, axis=1).reshape(
        slab_rows, model_width
    )
    expert_share = lax.psum_scatter(
        weighted.astype(jnp.bfloat16), "exp", scatter_dimension=1, tiled=True
    )
    return (stream_share.astype(jnp.bfloat16), expert_share)


def solution(mesh):
    placed = (
        P("ctx", "exp"),
        P("ctx", "exp"),
        P("ctx", None),
        P("ctx", None),
        P("exp", "ctx"),
        P("exp"),
        P("exp"),
        P("exp", None),
        P("ctx", None),
        P(),
        P(),
        P(None, "ctx", "exp"),
        P(None, "ctx", "exp"),
        P(None, "ctx", "exp"),
        P(),
    )
    return jax.shard_map(
        per_device,
        mesh=mesh,
        in_specs=placed,
        out_specs=(P("ctx", "exp"), P("ctx", "exp")),
        check_vma=False,
    )
```

profile of v0, /device:TPU:2, one launch (start us, length us, event | category | flops | bytes accessed | tf_op | source)
XLA Modules:
  0.0 1058.6 jit_solution(5072608627155439137)
XLA Ops:
  16.7 7.0 broadcast_select_fusion.2
  23.7 206.2 %all_to_all.45 = bf16[64,64,448]{2,1,0:T(8,128)(2,1)} all-to-all(bf16[64,64,448]{2,1,0:T(8,128)(2,1)S(1)} %get-tuple-element.53), channel_id=1, replica_groups=mesh['ctx'=32,'exp'=16] {'ctx'}, dimensions={0} | all-to-all | bytes 7340032 | tf_op jit(solution)/shard_map/all_to_all | solution.py:111
  229.9 195.0 %all_to_all.46 = bf16[64,64,448]{2,1,0:T(8,128)(2,1)} all-to-all(bf16[64,64,448]{2,1,0:T(8,128)(2,1)S(1)} %get-tuple-element.54), channel_id=1, replica_groups=mesh['ctx'=32,'exp'=16] {'ctx'}, dimensions={0} | all-to-all | bytes 7340032 | tf_op jit(solution)/shard_map/all_to_all | solution.py:112
  425.0 5.0 all-to-all-start.2
  431.3 364.5 %while.11 = (s32[]{:T(128)}, f32[4,64,128]{2,1,0:T(8,128)S(1)}, f32[1,4]{1,0:T(1,128)S(1)}, f32[4,64,128]{2,1,0:T(8,128)S(1)}, s32[]{:T(128)}, /*index=5*/s32[]{:T(128)}) while((s32[]{:T(128)}, f32[4,64,128]{2,1,0:T(8,128)S(1)}, f32[1,4]{1,0:T(1,128)S(1)}, f32[4,64,128]{2,1,0:T(8,128)S(1)}, s32[]{:T(128)}, ...), condition=%wide.region_2.3_spmd.clone, body=%wide.region_1.2_spmd.clone.sunk | while | flops 163843 | bytes 786567 | solution.py:74
  434.4 171.0 %collective-permute-start = (bf16[4,64,128]{2,1,0:T(8,128)(2,1)S(1)}, bf16[4,64,128]{2,1,0:T(8,128)(2,1)S(1)}, u32[]{:S(2)}, u32[]{:S(2)}) collective-permute-start(bf16[4,64,128]{2,1,0:T(8,128)(2,1)S(1)} %fusion.64), channel_id=1, source_target_pairs={{0,16},{16,32},{32,48},{48,64},{64,80},{80,96},{96,112},{112,128},... | collective-permute-start | bytes 196616 | tf_op jit(solution)/shard_map/while/body/eval_jaxpr/ppermute | solution.py:14
  606.4 10.2 collective-permute-start
  617.7 4.8 collective-permute-start
  623.5 4.7 collective-permute-start
  629.2 4.7 collective-permute-start
  634.9 4.7 collective-permute-start
  640.6 4.7 collective-permute-start
  646.3 4.7 collective-permute-start
  686.3 4.9 collective-permute-start
  692.2 5.9 collective-permute-start
  699.1 5.9 collective-permute-start
  706.0 5.9 collective-permute-start
  712.9 5.9 collective-permute-start
  719.8 5.9 collective-permute-start
  726.7 5.9 collective-permute-start
  733.7 5.9 collective-permute-start
  740.6 5.9 collective-permute-start
  747.5 5.9 collective-permute-start
  754.4 5.9 collective-permute-start
  761.3 5.9 collective-permute-start
  768.2 5.9 collective-permute-start
  775.2 5.9 collective-permute-start
  782.1 5.9 collective-permute-start
  789.0 5.9 collective-permute-start
  798.2 140.2 %all-reduce.2.cloned.1.call-done = bf16[128,2048]{1,0:T(8,128)(2,1)} async-done(((bf16[128,2048]{1,0:T(8,128)(2,1)}), bf16[128,2048]{1,0:T(8,128)(2,1)}) %all-reduce.2.cloned.1.call-update) | async-done | bytes 524304 | tf_op jit(solution)/shard_map/psum | solution.py:89
  954.2 7.9 fusion.2
  963.9 86.5 %reduce-scatter.4.cloned.1.call-done = bf16[128,128]{1,0:T(8,128)(2,1)} async-done(((bf16[2048,128]{1,0:T(8,128)(2,1)}), bf16[128,128]{1,0:T(8,128)(2,1)}) %reduce-scatter.4.cloned.1.call-update) | async-done | bytes 32784
  (180 shorter events, 92.5 us)
Async XLA Ops:
  425.0 524.6 %all-to-all-start.2 = ((bf16[64,64,448]{2,1,0:T(8,128)(2,1)}), bf16[64,64,448]{2,1,0:T(8,128)(2,1)}, u32[]{:S(2)}, u32[]{:S(2)}) async-start(bf16[64,64,448]{2,1,0:T(8,128)(2,1)} %get-tuple-element.55), calls=%async_computation.2 | async-start | bytes 8388608 | tf_op jit(solution)/shard_map/all_to_all | solution.py:113
  430.0 508.4 %all-reduce.2.cloned.1.call-start = ((), (), s32[]{:S(2)}) async-start(), calls=%async_computation.4 | async-start | bytes 1048576 | tf_op jit(solution)/shard_map/psum | solution.py:89
  434.4 171.9 %collective-permute-start = (bf16[4,64,128]{2,1,0:T(8,128)(2,1)S(1)}, bf16[4,64,128]{2,1,0:T(8,128)(2,1)S(1)}, u32[]{:S(2)}, u32[]{:S(2)}) collective-permute-start(bf16[4,64,128]{2,1,0:T(8,128)(2,1)S(1)} %fusion.64), channel_id=1, source_target_pairs={{0,16},{16,32},{32,48},{48,64},{64,80},{80,96},{96,112},{112,128},... | collective-permute-start | bytes 196616 | tf_op jit(solution)/shard_map/while/body/eval_jaxpr/ppermute | solution.py:14
  606.4 11.1 %collective-permute-start = (bf16[4,64,128]{2,1,0:T(8,128)(2,1)S(1)}, bf16[4,64,128]{2,1,0:T(8,128)(2,1)S(1)}, u32[]{:S(2)}, u32[]{:S(2)}) collective-permute-start(bf16[4,64,128]{2,1,0:T(8,128)(2,1)S(1)} %fusion.64), channel_id=1, source_target_pairs={{0,16},{16,32},{32,48},{48,64},{64,80},{80,96},{96,112},{112,128},... | collective-permute-start | bytes 196616 | tf_op jit(solution)/shard_map/while/body/eval_jaxpr/ppermute | solution.py:14
  617.7 5.7 collective-permute-start
  623.5 5.6 collective-permute-start
  629.2 5.6 collective-permute-start
  634.9 5.6 collective-permute-start
  640.6 5.6 collective-permute-start
  646.3 5.6 collective-permute-start
  652.1 5.6 collective-permute-start
  657.8 5.6 collective-permute-start
  663.5 5.6 collective-permute-start
  669.2 5.6 collective-permute-start
  674.9 5.6 collective-permute-start
  686.3 5.7 collective-permute-start
  692.2 6.8 collective-permute-start
  699.1 6.8 collective-permute-start
  706.0 6.8 collective-permute-start
  712.9 6.8 collective-permute-start
  719.8 6.8 collective-permute-start
  726.7 6.8 collective-permute-start
  733.7 6.8 collective-permute-start
  740.6 6.8 collective-permute-start
  747.5 6.8 collective-permute-start
  754.4 6.8 collective-permute-start
  761.3 6.8 collective-permute-start
  768.2 6.8 collective-permute-start
  775.2 6.8 collective-permute-start
  782.1 6.8 collective-permute-start
  789.0 6.8 collective-permute-start
  798.0 252.3 %reduce-scatter.4.cloned.1.call-start = ((), (), s32[]{:S(2)}) async-start(), calls=%async_computation.5 | async-start | bytes 557056
  (19 other events, 3421.5 us)
Sparse Core Ops, SparseCore 0:
  798.1 140.2 all-reduce.1
  963.2 87.0 reduce-scatter.3
where the time goes:
time: 1060 us
  blocking collectives  401 us (38%)
  starting transfers between devices  338 us (32%)
  waiting for transfers between devices  254 us (24%)
  local copies, waits for them, and re-layouts  24 us (2%)
  between operations  14.4 us (1%)
  other arithmetic  13.2 us (1%)
  matrix products  12.6 us (1%)
    ppermute x31, starting transfers between devices, shifted(): return lax.ppermute(shard, axis, pairs)  333 us
    all_to_all x1, blocking collectives, per_device(): lax.all_to_all(sent_gate, 'ctx', split_axis=0, concat_axis=1, tiled=True)  206 us
    all_to_all x1, blocking collectives, per_device(): lax.all_to_all(sent_up, 'ctx', split_axis=0, concat_axis=1, tiled=True)  195 us
    psum x1, waiting for transfers between devices, per_device(): mixed_sum = lax.psum(group_term, 'exp').astype(jnp.float32)  140 us
    unnamed x3, waiting for transfers between devices  86.5 us
    ppermute x31, waiting for transfers between devices, shifted(): return lax.ppermute(shard, axis, pairs)  27.3 us
  transfers between devices with their start and end apart: 34, of which 33 were waited for; matrix products, arithmetic and copies ran while one was open for 2% of the time, Pallas kernels for 0%

commit v1 on v0

--- a/solution.py
+++ b/solution.py
@@ -86,7 +86,7 @@
     model_width = residual.shape[1]
     share_cols = model_width // lax.axis_size("exp")
     first_col = lax.axis_index("exp") * share_cols
-    mixed_sum = lax.psum(group_term, "exp").astype(jnp.float32)
+    mixed_sum = jnp.sum(lax.all_gather(group_term, "exp"), axis=0).astype(jnp.float32)
     stream_full = mixed_sum + residual.astype(jnp.float32)
     mean_square = jnp.mean(stream_full * stream_full, axis=1, keepdims=True)
     normed = (stream_full * lax.rsqrt(mean_square + epsilon) * norm_gain).astype(jnp.bfloat16)

time: 1060 us -> 943 us (0.89)
  blocking collectives: 401 us -> 206 us
  starting transfers between devices: 338 us -> 374 us
  waiting for transfers between devices: 254 us -> 287 us
    all_to_all x1 -> x0, blocking collectives: 195 us -> none  [per_device(): lax.all_to_all(sent_up, 'ctx', split_axis=0, concat_axis=1, tiled=True)]
    all_to_all x1, waiting for transfers between devices: 0.01 us -> 173 us  [per_device(): lax.all_to_all(sent_down, 'ctx', split_axis=0, concat_axis=1, tiled=True)]
    psum x1 -> x0, waiting for transfers between devices: 140 us -> none  [per_device(): mixed_sum = lax.psum(group_term, 'exp').astype(jnp.float32)]
    all_to_all x1, starting transfers between devices: 5 us -> 36 us  [per_device(): lax.all_to_all(sent_down, 'ctx', split_axis=0, concat_axis=1, tiled=True)]
  transfers between devices with their start and end apart: 34 -> 35, of which waited for: 33 -> 33; matrix products, arithmetic and copies ran while one was open for 2% -> 2% of each run, Pallas kernels for 0% -> 0%
where the time goes in v1:
time: 943 us; the launch traced here: 942 us
  starting transfers between devices  374 us (40%)
  waiting for transfers between devices  287 us (30%)
  blocking collectives  206 us (22%)
  local copies, waits for them, and re-layouts  27.6 us (3%)
  other arithmetic  17.1 us (2%)
  matrix products  14.8 us (2%)
  between operations  14.4 us (2%)
    ppermute x31, starting transfers between devices, shifted(): return lax.ppermute(shard, axis, pairs)  333 us
    all_to_all x1, blocking collectives, per_device(): lax.all_to_all(sent_gate, 'ctx', split_axis=0, concat_axis=1, tiled=True)  206 us
    all_to_all x1, waiting for transfers between devices, per_device(): lax.all_to_all(sent_down, 'ctx', split_axis=0, concat_axis=1, tiled=True)  173 us
    unnamed x3, waiting for transfers between devices  85.8 us
    all_to_all x1, starting transfers between devices, per_device(): lax.all_to_all(sent_down, 'ctx', split_axis=0, concat_axis=1, tiled=True)  36 us
    ppermute x31, waiting for transfers between devices, shifted(): return lax.ppermute(shard, axis, pairs)  27.3 us
  transfers between devices with their start and end apart: 35, of which 33 were waited for; matrix products, arithmetic and copies ran while one was open for 2% of the time, Pallas kernels for 0%

profile of v1, /device:TPU:2, one launch (start us, length us, event | category | flops | bytes accessed | tf_op | source)
XLA Modules:
  0.0 942.1 jit_solution(11643341034983709818)
XLA Ops:
  16.7 7.7 broadcast_select_fusion.2
  24.4 206.2 %all_to_all.45 = bf16[64,64,448]{2,1,0:T(8,128)(2,1)} all-to-all(bf16[64,64,448]{2,1,0:T(8,128)(2,1)S(1)} %get-tuple-element.53), channel_id=1, replica_groups=mesh['ctx'=32,'exp'=16] {'ctx'}, dimensions={0} | all-to-all | bytes 7340032 | tf_op jit(solution)/shard_map/all_to_all | solution.py:111
  230.6 5.0 all-to-all-start.1
  236.9 364.6 %while.11 = (s32[]{:T(128)}, f32[4,64,128]{2,1,0:T(8,128)S(1)}, f32[1,4]{1,0:T(1,128)S(1)}, f32[4,64,128]{2,1,0:T(8,128)S(1)}, s32[]{:T(128)}, /*index=5*/s32[]{:T(128)}) while((s32[]{:T(128)}, f32[4,64,128]{2,1,0:T(8,128)S(1)}, f32[1,4]{1,0:T(1,128)S(1)}, f32[4,64,128]{2,1,0:T(8,128)S(1)}, s32[]{:T(128)}, ...), condition=%wide.region_2.3_spmd.clone, body=%wide.region_1.2_spmd.clone.sunk | while | flops 163843 | bytes 786567 | solution.py:74
  240.0 171.1 %collective-permute-start = (bf16[4,64,128]{2,1,0:T(8,128)(2,1)S(1)}, bf16[4,64,128]{2,1,0:T(8,128)(2,1)S(1)}, u32[]{:S(2)}, u32[]{:S(2)}) collective-permute-start(bf16[4,64,128]{2,1,0:T(8,128)(2,1)S(1)} %fusion.64), channel_id=1, source_target_pairs={{0,16},{16,32},{32,48},{48,64},{64,80},{80,96},{96,112},{112,128},... | collective-permute-start | bytes 196616 | tf_op jit(solution)/shard_map/while/body/eval_jaxpr/ppermute | solution.py:14
  412.1 10.2 %collective-permute-start = (bf16[4,64,128]{2,1,0:T(8,128)(2,1)S(1)}, bf16[4,64,128]{2,1,0:T(8,128)(2,1)S(1)}, u32[]{:S(2)}, u32[]{:S(2)}) collective-permute-start(bf16[4,64,128]{2,1,0:T(8,128)(2,1)S(1)} %fusion.64), channel_id=1, source_target_pairs={{0,16},{16,32},{32,48},{48,64},{64,80},{80,96},{96,112},{112,128},... | collective-permute-start | bytes 196616 | tf_op jit(solution)/shard_map/while/body/eval_jaxpr/ppermute | solution.py:14
  423.4 4.8 collective-permute-start
  429.2 4.7 collective-permute-start
  434.9 4.7 collective-permute-start
  440.6 4.7 collective-permute-start
  492.0 4.9 collective-permute-start
  497.9 5.9 collective-permute-start
  504.8 5.9 collective-permute-start
  511.7 5.9 collective-permute-start
  518.6 5.9 collective-permute-start
  525.5 5.9 collective-permute-start
  532.4 5.9 collective-permute-start
  539.4 5.9 collective-permute-start
  546.3 5.9 collective-permute-start
  553.2 5.9 collective-permute-start
  560.1 5.9 collective-permute-start
  567.0 5.9 collective-permute-start
  573.9 5.9 collective-permute-start
  580.9 5.9 collective-permute-start
  587.8 5.9 collective-permute-start
  594.7 5.9 collective-permute-start
  603.7 36.0 %all-to-all-start.2 = ((bf16[64,64,448]{2,1,0:T(8,128)(2,1)}), bf16[64,64,448]{2,1,0:T(8,128)(2,1)}, u32[]{:S(2)}, u32[]{:S(2)}) async-start(bf16[64,64,448]{2,1,0:T(8,128)(2,1)} %get-tuple-element.55), calls=%async_computation.2 | async-start | bytes 8388608 | tf_op jit(solution)/shard_map/all_to_all | solution.py:113
  644.8 4.9 copy.41
  649.7 173.5 %all-to-all-done.2 = bf16[64,64,448]{2,1,0:T(8,128)(2,1)} async-done(((bf16[64,64,448]{2,1,0:T(8,128)(2,1)}), bf16[64,64,448]{2,1,0:T(8,128)(2,1)}, u32[]{:S(2)}, u32[]{:S(2)}) %all-to-all-start.2) | async-done | bytes 3670048 | tf_op jit(solution)/shard_map/all_to_all | solution.py:113
  827.8 5.3 reduce_sum.30
  838.4 7.9 fusion.2
  848.1 85.7 %reduce-scatter.4.cloned.1.call-done = bf16[128,128]{1,0:T(8,128)(2,1)} async-done(((bf16[2048,128]{1,0:T(8,128)(2,1)}), bf16[128,128]{1,0:T(8,128)(2,1)}) %reduce-scatter.4.cloned.1.call-update) | async-done | bytes 32784
  (180 shorter events, 100.9 us)
Async XLA Ops:
  230.6 373.1 %all-to-all-start.1 = ((bf16[64,64,448]{2,1,0:T(8,128)(2,1)}), bf16[64,64,448]{2,1,0:T(8,128)(2,1)}, u32[]{:S(2)}, u32[]{:S(2)}) async-start(bf16[64,64,448]{2,1,0:T(8,128)(2,1)} %get-tuple-element.54), calls=%async_computation.1 | async-start | bytes 8388608 | tf_op jit(solution)/shard_map/all_to_all | solution.py:112
  235.7 592.1 %all-gather.3.cloned.1.call-start = ((), (), s32[]{:S(2)}) async-start(), calls=%async_computation.4 | async-start | bytes 8912896 | tf_op jit(solution)/shard_map/all_gather | solution.py:89
  240.0 172.0 %collective-permute-start = (bf16[4,64,128]{2,1,0:T(8,128)(2,1)S(1)}, bf16[4,64,128]{2,1,0:T(8,128)(2,1)S(1)}, u32[]{:S(2)}, u32[]{:S(2)}) collective-permute-start(bf16[4,64,128]{2,1,0:T(8,128)(2,1)S(1)} %fusion.64), channel_id=1, source_target_pairs={{0,16},{16,32},{32,48},{48,64},{64,80},{80,96},{96,112},{112,128},... | collective-permute-start | bytes 196616 | tf_op jit(solution)/shard_map/while/body/eval_jaxpr/ppermute | solution.py:14
  412.1 11.1 %collective-permute-start = (bf16[4,64,128]{2,1,0:T(8,128)(2,1)S(1)}, bf16[4,64,128]{2,1,0:T(8,128)(2,1)S(1)}, u32[]{:S(2)}, u32[]{:S(2)}) collective-permute-start(bf16[4,64,128]{2,1,0:T(8,128)(2,1)S(1)} %fusion.64), channel_id=1, source_target_pairs={{0,16},{16,32},{32,48},{48,64},{64,80},{80,96},{96,112},{112,128},... | collective-permute-start | bytes 196616 | tf_op jit(solution)/shard_map/while/body/eval_jaxpr/ppermute | solution.py:14
  423.4 5.7 collective-permute-start
  429.2 5.6 collective-permute-start
  434.9 5.6 collective-permute-start
  440.6 5.6 collective-permute-start
  446.3 5.6 collective-permute-start
  452.0 5.6 collective-permute-start
  457.7 5.6 collective-permute-start
  463.5 5.6 collective-permute-start
  469.2 5.6 collective-permute-start
  474.9 5.6 collective-permute-start
  492.0 5.7 collective-permute-start
  497.9 6.8 collective-permute-start
  504.8 6.8 collective-permute-start
  511.7 6.8 collective-permute-start
  518.6 6.8 collective-permute-start
  525.5 6.8 collective-permute-start
  532.4 6.8 collective-permute-start
  539.4 6.8 collective-permute-start
  546.3 6.8 collective-permute-start
  553.2 6.8 collective-permute-start
  560.1 6.8 collective-permute-start
  567.0 6.8 collective-permute-start
  573.9 6.8 collective-permute-start
  580.9 6.8 collective-permute-start
  587.8 6.8 collective-permute-start
  594.7 6.8 collective-permute-start
  603.7 219.5 %all-to-all-start.2 = ((bf16[64,64,448]{2,1,0:T(8,128)(2,1)}), bf16[64,64,448]{2,1,0:T(8,128)(2,1)}, u32[]{:S(2)}, u32[]{:S(2)}) async-start(bf16[64,64,448]{2,1,0:T(8,128)(2,1)} %get-tuple-element.55), calls=%async_computation.2 | async-start | bytes 8388608 | tf_op jit(solution)/shard_map/all_to_all | solution.py:113
  639.7 294.1 %reduce-scatter.4.cloned.1.call-start = ((), (), s32[]{:S(2)}) async-start(), calls=%async_computation.5 | async-start | bytes 557056
  (19 other events, 1668.6 us)
Sparse Core Ops, SparseCore 0:
  603.8 110.8 all-gather.2
  847.4 86.3 reduce-scatter.3
